TPU v7x, 32 devices: a whole 2x2x4 slice. The times are simulated.
32 devices in a mesh: slow: 8 (over y, x, core), fast: 4 (over z).
Axes of the slice: x: 2, y: 2, z: 4, core: 2. Of those that a mesh axis runs over, the one named last changes fastest.
Arguments:
- query_act: bfloat16 [4096, 512], P(('slow', 'fast')), may hold values from -6 to 6
- key_act: bfloat16 [4096, 512], P(('slow', 'fast')), may hold values from -6 to 6
- value_act: bfloat16 [4096, 512], P(('slow', 'fast')), may hold values from -6 to 6
- long_filter: bfloat16 [4096, 32], P(('slow', 'fast')), may hold values from -4 to 4
- out_grad: bfloat16 [4096, 512], P(('slow', 'fast')), may hold values from -6 to 6
Outputs:
- mixed_out: bfloat16 [4096, 512], P(('slow', 'fast'))
- query_grad: bfloat16 [4096, 512], P(('slow', 'fast'))
- key_grad: bfloat16 [4096, 512], P(('slow', 'fast'))
- value_grad: bfloat16 [4096, 512], P(('slow', 'fast'))
- filter_grad: float32 [4096, 32], P(('slow', 'fast'))
All inputs are finite; a program needn't handle non-finite values.
Results may differ from a plain program's by a relative error of at most 0.0049.
Values may be sent and summed in bfloat16 or wider, within the bound.
No kernel may reach another device: no remote copies, remote signals or barrier semaphores. Data moves between devices by JAX's collectives and lax.ppermute only.
A program may use at most 64 MiB of HBM per device.

v0:
```python
import functools
import math

import jax
import jax.numpy as jnp
from jax import lax
from jax.experimental import pallas as pl
from jax.experimental.pallas import tpu as pltpu
from jax.sharding import PartitionSpec as P

highest = lax.Precision.HIGHEST


def index_ramp(points, along, ndim, offset):
    shape_list = [1] * ndim
    shape_list[along] = points
    return (jnp.arange(points, dtype=jnp.int32) + offset).reshape(shape_list)


def apply_dft(re_im, points, direction, along):
    index_row = jnp.arange(points, dtype=jnp.int32)
    phase_turns = index_row[:, None] * index_row[None, :] % points
    phases = 2.0 * math.pi / points * phase_turns.astype(jnp.float32)
    cosine = jnp.cos(phases)
    sine_part = direction * jnp.sin(phases)

    def contract(values, matrix):
        result = jnp.tensordot(values, matrix, axes=((along,), (1,)), precision=highest)
        return jnp.moveaxis(result, -1, along)

    return (
        contract(re_im[0], cosine) - contract(re_im[1], sine_part),
        contract(re_im[0], sine_part) + contract(re_im[1], cosine),
    )


def rotate(re_im, phase_turns, period, direction):
    phases = 2.0 * math.pi / period * (phase_turns % period).astype(jnp.float32)
    cosine = jnp.cos(phases)
    sine_part = direction * jnp.sin(phases)
    return (re_im[0] * cosine - re_im[1] * sine_part, re_im[0] * sine_part + re_im[1] * cosine)


def complex_times(left, right):
    return (left[0] * right[0] - left[1] * right[1], left[0] * right[1] + left[1] * right[0])


def conj_times(left, right):
    return (left[0] * right[0] + left[1] * right[1], left[0] * right[1] - left[1] * right[0])


def positions(grid_info, slow_points, slow_offset, fast_points, fast_offset):
    fast_count, tokens = (grid_info[1], grid_info[2])
    block_index = index_ramp(slow_points, 2, 5, slow_offset) * fast_count + index_ramp(
        fast_points, 3, 5, fast_offset
    )
    return block_index * tokens + index_ramp(tokens, 4, 5, 0)


def open_halves(re_im, grid_info, fast_offset):
    token_place = positions(grid_info, re_im[0].shape[1], 0, re_im[0].shape[2], fast_offset)
    return rotate(
        (re_im[0][None], re_im[1][None]),
        index_ramp(2, 0, 5, 0) * token_place,
        2 * grid_info[3],
        -1.0,
    )


def fold_halves(re_im, token_place, seq_length):
    turned = rotate(re_im, index_ramp(2, 0, 5, 0) * token_place, 2 * seq_length, 1.0)
    scale = 0.5 / seq_length
    return (jnp.sum(turned[0], axis=0) * scale, jnp.sum(turned[1], axis=0) * scale)


def front_forward(re_im, grid_info, fast_offset):
    slow_count, fast_count = (grid_info[0], grid_info[1])
    re_im = apply_dft(re_im, slow_count, -1.0, 2)
    phase_turns = index_ramp(slow_count, 2, 5, 0) * index_ramp(re_im[0].shape[3], 3, 5, fast_offset)
    return rotate(re_im, phase_turns, slow_count * fast_count, -1.0)


def front_inverse(re_im, grid_info, fast_offset):
    slow_count, fast_count = (grid_info[0], grid_info[1])
    phase_turns = index_ramp(slow_count, 2, 5, 0) * index_ramp(re_im[0].shape[3], 3, 5, fast_offset)
    re_im = rotate(re_im, phase_turns, slow_count * fast_count, 1.0)
    return apply_dft(re_im, slow_count, 1.0, 2)


def lead_phase(re_im, grid_info, ka_offset):
    slow_count, fast_count, tokens = (grid_info[0], grid_info[1], grid_info[2])
    lead_index = index_ramp(re_im[0].shape[2], 2, 5, ka_offset) + slow_count * index_ramp(
        fast_count, 3, 5, 0
    )
    return lead_index * index_ramp(tokens, 4, 5, 0)


def back_forward(re_im, grid_info, ka_offset):
    re_im = apply_dft(re_im, grid_info[1], -1.0, 3)
    re_im = rotate(re_im, lead_phase(re_im, grid_info, ka_offset), grid_info[3], -1.0)
    return apply_dft(re_im, grid_info[2], -1.0, 4)


def back_inverse(re_im, grid_info, ka_offset):
    re_im = apply_dft(re_im, grid_info[2], 1.0, 4)
    re_im = rotate(re_im, lead_phase(re_im, grid_info, ka_offset), grid_info[3], 1.0)
    return apply_dft(re_im, grid_info[1], 1.0, 3)


def to_channels(seq_rows):
    return lax.all_to_all(
        seq_rows.reshape(1, seq_rows.shape[0], seq_rows.shape[1]),
        "slow",
        split_axis=2,
        concat_axis=0,
        tiled=True,
    )


def merge_blocks(arrays, block_count):
    tokens = arrays[0].shape[0]
    pieces = [item.reshape(tokens, block_count, item.shape[1] // block_count) for item in arrays]
    return jnp.concatenate(pieces, axis=2).reshape(tokens, -1)


def split_columns(rows_major, widths):
    tokens, block_count = (rows_major.shape[0], rows_major.shape[1])
    result = []
    offset = 0
    for length in widths:
        result.append(
            rows_major[:, :, offset : offset + length].reshape(tokens, block_count * length)
        )
        offset += length
    return result


def real_blocks(real_part, imag_part, segments):
    pieces = []
    offset = 0
    for output_kind, length in segments:
        real_seg = real_part[:, offset : offset + length]
        imag_seg = imag_part[:, offset : offset + length]
        offset += length
        if output_kind == "pairs":
            stacked = jnp.transpose(jnp.stack((real_seg, imag_seg), axis=-1), (0, 2, 1, 3))
            pieces.append(stacked.reshape(stacked.shape[0], stacked.shape[1], 2 * length))
        else:
            pieces.append(jnp.transpose(real_seg, (0, 2, 1)))
    return jnp.concatenate(pieces, axis=2)


def segment_widths(segments):
    return [2 * length if output_kind == "pairs" else length for output_kind, length in segments]


def spread_forward(seq_rows, grid_info, fast_rank, segments):
    slow_count, fast_count = (grid_info[0], grid_info[1])
    blocks = to_channels(seq_rows).astype(jnp.float32)
    real_list = []
    imag_list = []
    offset = 0
    for length, packed in segments:
        segment = blocks[:, :, offset : offset + length]
        offset += length
        if packed:
            halves = segment.reshape(segment.shape[0], segment.shape[1], length // 2, 2)
            real_seg, imag_seg = (halves[..., 0], halves[..., 1])
        else:
            real_seg, imag_seg = (segment, jnp.zeros_like(segment))
        real_list.append(jnp.transpose(real_seg, (2, 0, 1)))
        imag_list.append(jnp.transpose(imag_seg, (2, 0, 1)))
    re_im = (
        jnp.concatenate(real_list, 0)[:, :, None, :],
        jnp.concatenate(imag_list, 0)[:, :, None, :],
    )
    re_im = front_forward(open_halves(re_im, grid_info, fast_rank), grid_info, fast_rank)
    re_im = (
        lax.all_to_all(re_im[0], "fast", split_axis=2, concat_axis=3, tiled=True),
        lax.all_to_all(re_im[1], "fast", split_axis=2, concat_axis=3, tiled=True),
    )
    return back_forward(re_im, grid_info, fast_rank * (slow_count // fast_count))


def spread_inverse(re_im, grid_info, fast_rank, slow_rank, segments):
    slow_count, fast_count, tokens, seq_length = grid_info
    re_im = back_inverse(re_im, grid_info, fast_rank * (slow_count // fast_count))
    re_im = (
        lax.all_to_all(re_im[0], "fast", split_axis=3, concat_axis=2, tiled=True),
        lax.all_to_all(re_im[1], "fast", split_axis=3, concat_axis=2, tiled=True),
    )
    re_im = front_inverse(re_im, grid_info, fast_rank)
    re_im = (
        lax.all_to_all(re_im[0], "slow", split_axis=2, concat_axis=1, tiled=True),
        lax.all_to_all(re_im[1], "slow", split_axis=2, concat_axis=1, tiled=True),
    )
    real_part, imag_part = fold_halves(
        re_im, positions(grid_info, 1, slow_rank, 1, fast_rank), seq_length
    )
    length = real_part.shape[0] // slow_count
    blocks = real_blocks(
        real_part.reshape(slow_count, length, tokens),
        imag_part.reshape(slow_count, length, tokens),
        segments,
    )
    rows_major = jnp.transpose(blocks, (1, 0, 2))
    return split_columns(rows_major, segment_widths(segments))


def regroup(re_im, length, local_groups):

    def by_group(values):
        values = values[:, :length]
        return values.reshape(
            (values.shape[0], local_groups, length // local_groups) + values.shape[2:]
        )

    return (by_group(re_im[0]), by_group(re_im[1]))


def flatten_pairs(re_im):

    def merged(values):
        return values.reshape(
            (values.shape[0], values.shape[1] * values.shape[2]) + values.shape[3:]
        )

    return (merged(re_im[0]), merged(re_im[1]))


def by_spectra(query_act, key_act, value_act, long_filter, out_grad):
    tokens, channels = query_act.shape
    groups = long_filter.shape[1]
    slow_count = lax.axis_size("slow")
    fast_count = lax.axis_size("fast")
    seq_length = tokens * slow_count * fast_count
    grid_info = (slow_count, fast_count, tokens, seq_length)
    group_width = channels // groups
    product = (key_act.astype(jnp.float32) * value_act.astype(jnp.float32)).astype(jnp.bfloat16)
    grad_in = (out_grad.astype(jnp.float32) * query_act.astype(jnp.float32)).astype(jnp.bfloat16)
    fast_rank = lax.axis_index("fast")
    slow_rank = lax.axis_index("slow")
    data_pairs = channels // (2 * slow_count)
    local_groups = groups // slow_count
    block_width = channels // slow_count
    spectra = spread_forward(
        merge_blocks((product, long_filter), slow_count),
        grid_info,
        fast_rank,
        ((block_width, True), (local_groups, False)),
    )
    prod_spec = regroup(spectra, data_pairs, local_groups)
    filter_spec = (spectra[0][:, data_pairs:, None], spectra[1][:, data_pairs:, None])
    convolved = spread_inverse(
        flatten_pairs(complex_times(prod_spec, filter_spec)),
        grid_info,
        fast_rank,
        slow_rank,
        (("pairs", data_pairs),),
    )[0]
    grad_spec = regroup(
        spread_forward(grad_in, grid_info, fast_rank, ((block_width, True),)),
        data_pairs,
        local_groups,
    )
    back_spec = flatten_pairs(conj_times(filter_spec, grad_spec))
    corr_spec = conj_times(prod_spec, grad_spec)
    joined = (
        jnp.concatenate((back_spec[0], jnp.sum(corr_spec[0], axis=2)), axis=1),
        jnp.concatenate((back_spec[1], jnp.sum(corr_spec[1], axis=2)), axis=1),
    )
    backward, filter_sum = spread_inverse(
        joined, grid_info, fast_rank, slow_rank, (("pairs", data_pairs), ("real", local_groups))
    )
    scale = 1.0 / math.sqrt(seq_length * group_width)
    mixed_out = (query_act.astype(jnp.float32) * convolved).astype(jnp.bfloat16)
    query_grad = (out_grad.astype(jnp.float32) * convolved).astype(jnp.bfloat16)
    key_grad = (backward * value_act.astype(jnp.float32)).astype(jnp.bfloat16)
    value_grad = (backward * key_act.astype(jnp.float32)).astype(jnp.bfloat16)
    return (mixed_out, query_grad, key_grad, value_grad, filter_sum * scale)


f32 = jnp.float32
bf16 = jnp.bfloat16
EXTRA_ROWS = 2


def dot(left, right):
    return jnp.dot(left, right, preferred_element_type=f32)


def dot_nt(left, right):
    return lax.dot_general(left, right, (((1,), (1,)), ((), ())), preferred_element_type=f32)


def ramp(shape, dim):
    return lax.broadcasted_iota(jnp.int32, shape, dim)


def flip_matrix(size):
    return (ramp((size, size), 0) + ramp((size, size), 1) == size - 1).astype(bf16)


def eye_matrix(size):
    return (ramp((size, size), 0) == ramp((size, size), 1)).astype(bf16)


def gate_kernel(query, key, value, filt, grad, sent, queries, keys, values, taps, grads, done):
    copies = [
        pltpu.make_async_copy(source, target, done.at[at])
        for at, (source, target) in enumerate(
            ((grad, grads), (query, queries), (key, keys), (value, values), (filt, taps))
        )
    ]
    for copy in copies:
        copy.start()
    tokens, channels = queries.shape
    groups = taps.shape[0]
    width = channels // groups
    rows = 2 * width + EXTRA_ROWS
    for copy in copies:
        copy.wait()
    grad_in = (grads[...].astype(f32) * queries[...].astype(f32)).astype(bf16)
    flipped = dot(flip_matrix(tokens), grad_in)
    product = (keys[...].astype(f32) * values[...].astype(f32)).astype(bf16)
    columns = product.astype(f32).T.astype(bf16)
    flipped = flipped.T.astype(bf16)
    for group in range(groups):
        at = group * rows
        part = slice(group * width, (group + 1) * width)
        sent[at : at + width, :] = columns[part]
        sent[at + width : at + 2 * width, :] = flipped[part]
        sent[at + 2 * width : at + rows, :] = jnp.broadcast_to(
            taps[group : group + 1, :], (EXTRA_ROWS, tokens)
        )


def group_kernel(scale, width, got, sent, streams, padded, toeplitz):
    rows, tokens = 2 * width + EXTRA_ROWS, got.shape[1]
    blocks = got.shape[0] // rows
    pairs = blocks // 2
    row, lane = ramp((tokens, tokens), 0), ramp((tokens, tokens), 1)
    for pair in range(pairs):
        for half in range(2):
            block = 2 * pair + half
            lanes = slice(half * tokens, (half + 1) * tokens)
            at = 2 * width * pair
            streams[at : at + width, lanes] = got[block * rows : block * rows + width, :]
            streams[at + width : at + 2 * width, lanes] = got[
                (blocks - 1 - block) * rows + width : (blocks - 1 - block) * rows + 2 * width, :
            ]
    for block in range(blocks):
        padded[block * width : (block + 1) * width, :] = got[
            block * rows + width : block * rows + 2 * width, :
        ]
    padded[blocks * width :, :] = jnp.zeros((blocks * width, tokens), bf16)

    before = jnp.zeros((tokens, tokens), f32)
    for block in range(blocks):
        taps = jnp.broadcast_to(got[block * rows + 2 * width : block * rows + 2 * width + 1, :].astype(f32), (tokens, tokens))
        turned = pltpu.roll(taps, 0, 1, stride=1, stride_axis=0)
        toeplitz[block] = jnp.where(lane >= row, turned, before).astype(bf16)
        before = turned

    total = None
    for pair in range(pairs):
        left = jnp.zeros((tokens, tokens), bf16) if pair == 0 else toeplitz[2 * pair - 1]
        weights = jnp.concatenate(
            (
                jnp.concatenate((toeplitz[2 * pair], toeplitz[2 * pair + 1]), axis=1),
                jnp.concatenate((left, toeplitz[2 * pair]), axis=1),
            ),
            axis=0,
        )
        skip = 2 * width * pair
        term = dot(streams[0 : 2 * width * pairs - skip, :], weights)
        total = term if pair == 0 else jnp.concatenate((total[:skip], total[skip:] + term), axis=0)
    for pair in range(pairs):
        for half in range(2):
            block = 2 * pair + half
            lanes = slice(half * tokens, (half + 1) * tokens)
            at = 2 * width * pair
            sent[block * rows : block * rows + width, :] = total[at : at + width, lanes].astype(bf16)
            place = (blocks - 1 - block) * rows + width
            sent[place : place + width, :] = total[
                at + width : at + 2 * width, lanes
            ].astype(bf16)

    ordered = jnp.concatenate(
        [got[block * rows : block * rows + width, :] for block in range(blocks)], axis=0
    )
    ordered = ordered.astype(f32).T.astype(bf16)
    carry = jnp.zeros((8, tokens), f32)
    which = ramp((EXTRA_ROWS, tokens), 0)
    for pair in range(pairs):
        depth = blocks * width if 2 * pair + 2 > blocks // 2 else blocks * width // 2
        columns = [
            padded[pl.ds((blocks - 1 - lag) * width, depth), :] for lag in (2 * pair, 2 * pair + 1)
        ]
        outer = dot(ordered[:, :depth], jnp.concatenate(columns, axis=1))
        for half in range(2):
            block = 2 * pair + half
            turned = pltpu.roll(
                outer[:, half * tokens : (half + 1) * tokens], 0, 1, stride=1, stride_axis=0
            )
            here = jnp.where(lane >= row, turned, 0.0).reshape(tokens // 8, 8, tokens).sum(axis=0)
            later = jnp.where(lane >= row, 0.0, turned).reshape(tokens // 8, 8, tokens).sum(axis=0)
            value = jnp.sum(here + carry, axis=0, keepdims=True) * scale
            carry = later
            high = value.astype(bf16).astype(f32)
            pieces = jnp.where(which == 0, high, jnp.where(which == 1, value - high, 0.0))
            place = (blocks - 1 - block) * rows + 2 * width
            sent[place : place + EXTRA_ROWS, :] = pieces.astype(bf16)


def output_kernel(
    width, got, query, key, value, grad, mixed, query_grad, key_grad, value_grad, filter_grad
):
    rows, tokens = 2 * width + EXTRA_ROWS, got.shape[1]
    blocks = got.shape[0] // rows

    def collect(first, count):
        return jnp.concatenate(
            [got[at * rows + first : at * rows + first + count, :] for at in range(blocks)], axis=0
        )

    flip = flip_matrix(tokens)
    convolved = dot_nt(eye_matrix(tokens), collect(0, width))
    mixed[...] = (query[...].astype(f32) * convolved).astype(bf16)
    query_grad[...] = (grad[...].astype(f32) * convolved).astype(bf16)
    backward = dot_nt(flip, collect(width, width))
    key_grad[...] = (backward * value[...].astype(f32)).astype(bf16)
    value_grad[...] = (backward * key[...].astype(f32)).astype(bf16)
    high, low = collect(2 * width, 1), collect(2 * width + 1, 1)
    filter_grad[...] = dot(high, flip) + dot(low, flip)


def by_groups(query_act, key_act, value_act, long_filter, out_grad):
    tokens, channels = query_act.shape
    groups = long_filter.shape[1]
    width = channels // groups
    rows = 2 * width + EXTRA_ROWS
    scale = 1.0 / math.sqrt(tokens * groups * width)
    chunks = jax.ShapeDtypeStruct((groups * rows, tokens), bf16)

    def exchange(sent):
        pieces = sent.reshape(groups, rows // 2, 2, tokens)
        pieces = lax.all_to_all(pieces, ("slow", "fast"), split_axis=0, concat_axis=0, tiled=True)
        return pieces.reshape(groups * rows, tokens)

    act = pltpu.VMEM((tokens, channels), bf16)
    sent = pl.pallas_call(
        gate_kernel,
        out_shape=chunks,
        in_specs=[pl.BlockSpec(memory_space=pltpu.HBM)] * 5,
        scratch_shapes=[
            act,
            act,
            act,
            pltpu.VMEM((groups, tokens), bf16),
            act,
            pltpu.SemaphoreType.DMA((5,)),
        ],
        compiler_params=pltpu.CompilerParams(vmem_limit_bytes=8 * 2**20),
        name="gate",
    )(
        *(
            pltpu.with_memory_space_constraint(array, pltpu.HBM)
            for array in (query_act, key_act, value_act, long_filter.T, out_grad)
        )
    )
    got = exchange(sent)
    sent = pl.pallas_call(
        functools.partial(group_kernel, scale, width),
        out_shape=chunks,
        scratch_shapes=[
            pltpu.VMEM((channels, 2 * tokens), bf16),
            pltpu.VMEM((2 * channels, tokens), bf16),
            pltpu.VMEM((groups, tokens, tokens), bf16),
        ],
        compiler_params=pltpu.CompilerParams(vmem_limit_bytes=16 * 2**20),
        name="group",
    )(got)
    got = exchange(sent)
    like = jax.ShapeDtypeStruct((tokens, channels), bf16)
    *acts, filter_grad = pl.pallas_call(
        functools.partial(output_kernel, width),
        out_shape=(like, like, like, like, jax.ShapeDtypeStruct((groups, tokens), f32)),
        compiler_params=pltpu.CompilerParams(vmem_limit_bytes=8 * 2**20),
        name="outputs",
    )(got, query_act, key_act, value_act, out_grad)
    return (*acts, filter_grad.T)


def on_device(query_act, key_act, value_act, long_filter, out_grad):
    tokens, channels = query_act.shape
    groups = long_filter.shape[1]
    devices = lax.axis_size("slow") * lax.axis_size("fast")
    if devices == groups and tokens == 128 and channels == 16 * groups and groups % 4 == 0:
        return by_groups(query_act, key_act, value_act, long_filter, out_grad)
    return by_spectra(query_act, key_act, value_act, long_filter, out_grad)


def solution(mesh):
    placed = (
        P(("slow", "fast"), None),
        P(("slow", "fast"), None),
        P(("slow", "fast"), None),
        P(("slow", "fast"), None),
        P(("slow", "fast"), None),
    )
    return jax.shard_map(
        on_device,
        mesh=mesh,
        in_specs=placed,
        out_specs=(
            P(("slow", "fast"), None),
            P(("slow", "fast"), None),
            P(("slow", "fast"), None),
            P(("slow", "fast"), None),
            P(("slow", "fast"), None),
        ),
        check_vma=False,
    )
```

profile of v0, /device:TPU:1, one launch (start us, length us, event | category | flops | bytes accessed | tf_op | source)
XLA Modules:
  0.0 35.1 jit_solution(14190328465523568648)
XLA Ops:
  0.6 1.4 %gate.1 = bf16[1088,128]{1,0:T(8,128)(2,1)S(1)} custom-call(bf16[128,512]{1,0:T(8,128)(2,1)} %query.3, bf16[128,512]{1,0:T(8,128)(2,1)} %key.3, bf16[128,512]{1,0:T(8,128)(2,1)} %value.3, bf16[32,128]{1,0:T(8,128)(2,1)} %bitcast.10, bf16[128,512]{1,0:T(8,128)(2,1)} %grad.3), custom_call_target="tpu_custom_call" | custom-call | tf_op jit(solution)/shard_map/gate/pallas_call | solution.py:452
  2.1 17.6 %all_to_all.10 = bf16[32,17,2,128]{3,2,1,0:T(2,128)(2,1)S(1)} all-to-all(bf16[32,17,2,128]{3,2,1,0:T(2,128)(2,1)S(1)} %bitcast.9), channel_id=1, replica_groups=mesh['slow'=8,'fast'=4] {'slow','fast'}, dimensions={0} | all-to-all | bytes 557056 | tf_op jit(solution)/shard_map/all_to_all | solution.py:448
  19.6 1.4 %group.1 = bf16[1088,128]{1,0:T(8,128)(2,1)S(1)} custom-call(bf16[1088,128]{1,0:T(8,128)(2,1)S(1)} %bitcast.7), custom_call_target="tpu_custom_call" | custom-call | tf_op jit(solution)/shard_map/group/pallas_call | solution.py:473
  21.0 0.0 copy-start
  21.0 0.0 copy-start.1
  21.0 0.0 copy-start.2
  21.0 0.0 copy-start.3
  21.1 13.1 %all_to_all.11 = bf16[32,17,2,128]{3,2,1,0:T(2,128)(2,1)S(1)} all-to-all(bf16[32,17,2,128]{3,2,1,0:T(2,128)(2,1)S(1)} %bitcast.8), channel_id=1, replica_groups=mesh['slow'=8,'fast'=4] {'slow','fast'}, dimensions={0} | all-to-all | bytes 557056 | tf_op jit(solution)/shard_map/all_to_all | solution.py:448
  34.1 0.0 copy-done
  34.1 0.0 copy-done.1
  34.1 0.0 copy-done.2
  34.1 0.0 copy-done.3
  34.2 1.0 %outputs.1 = (bf16[128,512]{1,0:T(8,128)(2,1)}, bf16[128,512]{1,0:T(8,128)(2,1)}, bf16[128,512]{1,0:T(8,128)(2,1)}, bf16[128,512]{1,0:T(8,128)(2,1)}, f32[32,128]{1,0:T(8,128)}) custom-call(bf16[1088,128]{1,0:T(8,128)(2,1)S(1)} %bitcast.6, bf16[128,512]{1,0:T(8,128)(2,1)S(1)} %copy-done, bf16[128,512]{1,0:T(8,128)(2,1)S(1)} %copy-done.1, ...), custom_call_target="tpu_custom_call" | custom-call | tf_op jit(solution)/shard_map/outputs/pallas_call | solution.py:486
Async XLA Ops:
  21.0 13.1 %copy-start = (bf16[128,512]{1,0:T(8,128)(2,1)S(1)}, bf16[128,512]{1,0:T(8,128)(2,1)}, u32[]{:S(2)}) copy-start(bf16[128,512]{1,0:T(8,128)(2,1)} %query.3) | copy-start | bytes 393220
  21.0 13.1 %copy-start.1 = (bf16[128,512]{1,0:T(8,128)(2,1)S(1)}, bf16[128,512]{1,0:T(8,128)(2,1)}, u32[]{:S(2)}) copy-start(bf16[128,512]{1,0:T(8,128)(2,1)} %key.3) | copy-start | bytes 393220
  21.0 13.1 %copy-start.2 = (bf16[128,512]{1,0:T(8,128)(2,1)S(1)}, bf16[128,512]{1,0:T(8,128)(2,1)}, u32[]{:S(2)}) copy-start(bf16[128,512]{1,0:T(8,128)(2,1)} %value.3) | copy-start | bytes 393220
  21.0 13.1 %copy-start.3 = (bf16[128,512]{1,0:T(8,128)(2,1)S(1)}, bf16[128,512]{1,0:T(8,128)(2,1)}, u32[]{:S(2)}) copy-start(bf16[128,512]{1,0:T(8,128)(2,1)} %grad.3) | copy-start | bytes 393220
where the time goes:
time: 35.3 us; the launch traced here: 35.1 us
  blocking collectives  30.6 us (87%)
  Pallas kernels  3.79 us (11%)
  between operations  0.69 us (2%)
    all_to_all x2, blocking collectives, exchange(): lax.all_to_all(pieces, ('slow', 'fast'), split_axis=0, concat_axis=0, til...  30.6 us
    pallas_call x1, Pallas kernels, by_groups(): pl.pallas_call(gate_kernel, out_shape=chunks, in_specs=[pl.BlockSpec(memo...  1.42 us
    pallas_call x1, Pallas kernels, by_groups(): pl.pallas_call(functools.partial(group_kernel, scale, width), out_shape=c...  1.38 us
    pallas_call x1, Pallas kernels, by_groups(): pl.pallas_call(functools.partial(output_kernel, width), out_shape=(like,...  0.99 us

commit v1 on v0

--- a/solution.py
+++ b/solution.py
@@ -306,12 +306,20 @@
 
 
 def gate_kernel(query, key, value, filt, grad, sent, queries, keys, values, taps, grads, done):
+    parts = 2
+    span = queries.shape[0] // parts
     copies = [
-        pltpu.make_async_copy(source, target, done.at[at])
+        pltpu.make_async_copy(
+            source.at[pl.ds(part * span, span), :],
+            target.at[pl.ds(part * span, span), :],
+            done.at[parts * at + part],
+        )
+        for part in range(parts)
         for at, (source, target) in enumerate(
-            ((grad, grads), (query, queries), (key, keys), (value, values), (filt, taps))
+            ((grad, grads), (query, queries), (key, keys), (value, values))
         )
     ]
+    copies.append(pltpu.make_async_copy(filt, taps, done.at[len(copies)]))
     for copy in copies:
         copy.start()
     tokens, channels = queries.shape
@@ -459,7 +467,7 @@
             act,
             pltpu.VMEM((groups, tokens), bf16),
             act,
-            pltpu.SemaphoreType.DMA((5,)),
+            pltpu.SemaphoreType.DMA((9,)),
         ],
         compiler_params=pltpu.CompilerParams(vmem_limit_bytes=8 * 2**20),
         name="gate",

time: 35.3 us -> 35.4 us (level)
  no operation moved by 1% of the time
where the time goes in v1:
time: 35.4 us; the launch traced here: 35.1 us
  blocking collectives  30.6 us (86%)
  Pallas kernels  3.79 us (11%)
  between operations  0.69 us (2%)
    all_to_all x2, blocking collectives, exchange(): lax.all_to_all(pieces, ('slow', 'fast'), split_axis=0, concat_axis=0, til...  30.6 us
    pallas_call x1, Pallas kernels, by_groups(): pl.pallas_call(gate_kernel, out_shape=chunks, in_specs=[pl.BlockSpec(memo...  1.43 us
    pallas_call x1, Pallas kernels, by_groups(): pl.pallas_call(functools.partial(group_kernel, scale, width), out_shape=c...  1.38 us
    pallas_call x1, Pallas kernels, by_groups(): pl.pallas_call(functools.partial(output_kernel, width), out_shape=(like,...  0.99 us

profile of v1, /device:TPU:1, one launch (start us, length us, event | category | flops | bytes accessed | tf_op | source)
XLA Modules:
  0.0 35.1 jit_solution(2707372643139544390)
XLA Ops:
  0.6 1.4 %gate.1 = bf16[1088,128]{1,0:T(8,128)(2,1)S(1)} custom-call(bf16[128,512]{1,0:T(8,128)(2,1)} %query.3, bf16[128,512]{1,0:T(8,128)(2,1)} %key.3, bf16[128,512]{1,0:T(8,128)(2,1)} %value.3, bf16[32,128]{1,0:T(8,128)(2,1)} %bitcast.10, bf16[128,512]{1,0:T(8,128)(2,1)} %grad.3), custom_call_target="tpu_custom_call" | custom-call | tf_op jit(solution)/shard_map/gate/pallas_call | solution.py:460
  2.1 17.6 %all_to_all.10 = bf16[32,17,2,128]{3,2,1,0:T(2,128)(2,1)S(1)} all-to-all(bf16[32,17,2,128]{3,2,1,0:T(2,128)(2,1)S(1)} %bitcast.9), channel_id=1, replica_groups=mesh['slow'=8,'fast'=4] {'slow','fast'}, dimensions={0} | all-to-all | bytes 557056 | tf_op jit(solution)/shard_map/all_to_all | solution.py:456
  19.6 1.4 %group.1 = bf16[1088,128]{1,0:T(8,128)(2,1)S(1)} custom-call(bf16[1088,128]{1,0:T(8,128)(2,1)S(1)} %bitcast.7), custom_call_target="tpu_custom_call" | custom-call | tf_op jit(solution)/shard_map/group/pallas_call | solution.py:481
  21.0 0.0 copy-start
  21.0 0.0 copy-start.1
  21.0 0.0 copy-start.2
  21.1 0.0 copy-start.3
  21.1 13.1 %all_to_all.11 = bf16[32,17,2,128]{3,2,1,0:T(2,128)(2,1)S(1)} all-to-all(bf16[32,17,2,128]{3,2,1,0:T(2,128)(2,1)S(1)} %bitcast.8), channel_id=1, replica_groups=mesh['slow'=8,'fast'=4] {'slow','fast'}, dimensions={0} | all-to-all | bytes 557056 | tf_op jit(solution)/shard_map/all_to_all | solution.py:456
  34.1 0.0 copy-done
  34.1 0.0 copy-done.1
  34.1 0.0 copy-done.2
  34.1 0.0 copy-done.3
  34.2 1.0 %outputs.1 = (bf16[128,512]{1,0:T(8,128)(2,1)}, bf16[128,512]{1,0:T(8,128)(2,1)}, bf16[128,512]{1,0:T(8,128)(2,1)}, bf16[128,512]{1,0:T(8,128)(2,1)}, f32[32,128]{1,0:T(8,128)}) custom-call(bf16[1088,128]{1,0:T(8,128)(2,1)S(1)} %bitcast.6, bf16[128,512]{1,0:T(8,128)(2,1)S(1)} %copy-done, bf16[128,512]{1,0:T(8,128)(2,1)S(1)} %copy-done.1, ...), custom_call_target="tpu_custom_call" | custom-call | tf_op jit(solution)/shard_map/outputs/pallas_call | solution.py:494
Async XLA Ops:
  21.0 13.1 %copy-start = (bf16[128,512]{1,0:T(8,128)(2,1)S(1)}, bf16[128,512]{1,0:T(8,128)(2,1)}, u32[]{:S(2)}) copy-start(bf16[128,512]{1,0:T(8,128)(2,1)} %query.3) | copy-start | bytes 393220
  21.0 13.1 %copy-start.1 = (bf16[128,512]{1,0:T(8,128)(2,1)S(1)}, bf16[128,512]{1,0:T(8,128)(2,1)}, u32[]{:S(2)}) copy-start(bf16[128,512]{1,0:T(8,128)(2,1)} %key.3) | copy-start | bytes 393220
  21.0 13.1 %copy-start.2 = (bf16[128,512]{1,0:T(8,128)(2,1)S(1)}, bf16[128,512]{1,0:T(8,128)(2,1)}, u32[]{:S(2)}) copy-start(bf16[128,512]{1,0:T(8,128)(2,1)} %value.3) | copy-start | bytes 393220
  21.1 13.1 %copy-start.3 = (bf16[128,512]{1,0:T(8,128)(2,1)S(1)}, bf16[128,512]{1,0:T(8,128)(2,1)}, u32[]{:S(2)}) copy-start(bf16[128,512]{1,0:T(8,128)(2,1)} %grad.3) | copy-start | bytes 393220

commit v2 on v0

--- a/solution.py
+++ b/solution.py
@@ -335,6 +335,10 @@
         )
 
 
+def turn(square):
+    return pltpu.roll(square, 0, 1, stride=1, stride_axis=0)
+
+
 def group_kernel(scale, width, got, sent, streams, padded, toeplitz):
     rows, tokens = 2 * width + EXTRA_ROWS, got.shape[1]
     blocks = got.shape[0] // rows
@@ -355,12 +359,33 @@
         ]
     padded[blocks * width :, :] = jnp.zeros((blocks * width, tokens), bf16)
 
+    ordered = jnp.concatenate(
+        [got[block * rows : block * rows + width, :] for block in range(blocks)], axis=0
+    )
+    ordered = ordered.astype(f32).T.astype(bf16)
+    band = jnp.zeros((tokens, tokens), f32)
     before = jnp.zeros((tokens, tokens), f32)
-    for block in range(blocks):
-        taps = jnp.broadcast_to(got[block * rows + 2 * width : block * rows + 2 * width + 1, :].astype(f32), (tokens, tokens))
-        turned = pltpu.roll(taps, 0, 1, stride=1, stride_axis=0)
-        toeplitz[block] = jnp.where(lane >= row, turned, before).astype(bf16)
-        before = turned
+    which = ramp((EXTRA_ROWS, tokens), 0)
+    for pair in range(pairs):
+        depth = -(-2 * (pair + 1) * width // tokens) * tokens
+        columns = [
+            padded[pl.ds((blocks - 1 - lag) * width, depth), :] for lag in (2 * pair, 2 * pair + 1)
+        ]
+        outer = dot(ordered[:, :depth], jnp.concatenate(columns, axis=1))
+        for half in range(2):
+            block = 2 * pair + half
+            taps = got[block * rows + 2 * width : block * rows + 2 * width + 1, :].astype(f32)
+            turned = turn(jnp.broadcast_to(taps, (tokens, tokens)))
+            toeplitz[block] = jnp.where(lane >= row, turned, band).astype(bf16)
+            band = turned
+            turned = turn(outer[:, half * tokens : (half + 1) * tokens])
+            joined = jnp.where(lane >= row, turned, before)
+            before = turned
+            value = jnp.sum(joined, axis=0, keepdims=True) * scale
+            high = value.astype(bf16).astype(f32)
+            pieces = jnp.where(which == 0, high, value - high)
+            place = (blocks - 1 - block) * rows + 2 * width
+            sent[place : place + EXTRA_ROWS, :] = pieces.astype(bf16)
 
     total = None
     for pair in range(pairs):
@@ -385,32 +410,6 @@
             sent[place : place + width, :] = total[
                 at + width : at + 2 * width, lanes
             ].astype(bf16)
-
-    ordered = jnp.concatenate(
-        [got[block * rows : block * rows + width, :] for block in range(blocks)], axis=0
-    )
-    ordered = ordered.astype(f32).T.astype(bf16)
-    carry = jnp.zeros((8, tokens), f32)
-    which = ramp((EXTRA_ROWS, tokens), 0)
-    for pair in range(pairs):
-        depth = blocks * width if 2 * pair + 2 > blocks // 2 else blocks * width // 2
-        columns = [
-            padded[pl.ds((blocks - 1 - lag) * width, depth), :] for lag in (2 * pair, 2 * pair + 1)
-        ]
-        outer = dot(ordered[:, :depth], jnp.concatenate(columns, axis=1))
-        for half in range(2):
-            block = 2 * pair + half
-            turned = pltpu.roll(
-                outer[:, half * tokens : (half + 1) * tokens], 0, 1, stride=1, stride_axis=0
-            )
-            here = jnp.where(lane >= row, turned, 0.0).reshape(tokens // 8, 8, tokens).sum(axis=0)
-            later = jnp.where(lane >= row, 0.0, turned).reshape(tokens // 8, 8, tokens).sum(axis=0)
-            value = jnp.sum(here + carry, axis=0, keepdims=True) * scale
-            carry = later
-            high = value.astype(bf16).astype(f32)
-            pieces = jnp.where(which == 0, high, jnp.where(which == 1, value - high, 0.0))
-            place = (blocks - 1 - block) * rows + 2 * width
-            sent[place : place + EXTRA_ROWS, :] = pieces.astype(bf16)
 
 
 def output_kernel(

time: 35.3 us -> 35.2 us (level)
  no operation moved by 1% of the time
where the time goes in v2:
time: 35.2 us; the launch traced here: 35.1 us
  blocking collectives  30.6 us (87%)
  Pallas kernels  3.7 us (11%)
  between operations  0.69 us (2%)
    all_to_all x2, blocking collectives, exchange(): lax.all_to_all(pieces, ('slow', 'fast'), split_axis=0, concat_axis=0, til...  30.6 us
    pallas_call x1, Pallas kernels, by_groups(): pl.pallas_call(gate_kernel, out_shape=chunks, in_specs=[pl.BlockSpec(memo...  1.42 us
    pallas_call x1, Pallas kernels, by_groups(): pl.pallas_call(functools.partial(group_kernel, scale, width), out_shape=c...  1.29 us
    pallas_call x1, Pallas kernels, by_groups(): pl.pallas_call(functools.partial(output_kernel, width), out_shape=(like,...  0.99 us

profile of v2, /device:TPU:1, one launch (start us, length us, event | category | flops | bytes accessed | tf_op | source)
XLA Modules:
  0.0 35.1 jit_solution(6975954853051310015)
XLA Ops:
  0.6 1.4 %gate.1 = bf16[1088,128]{1,0:T(8,128)(2,1)S(1)} custom-call(bf16[128,512]{1,0:T(8,128)(2,1)} %query.3, bf16[128,512]{1,0:T(8,128)(2,1)} %key.3, bf16[128,512]{1,0:T(8,128)(2,1)} %value.3, bf16[32,128]{1,0:T(8,128)(2,1)} %bitcast.10, bf16[128,512]{1,0:T(8,128)(2,1)} %grad.3), custom_call_target="tpu_custom_call" | custom-call | tf_op jit(solution)/shard_map/gate/pallas_call | solution.py:451
  2.1 17.6 %all_to_all.10 = bf16[32,17,2,128]{3,2,1,0:T(2,128)(2,1)S(1)} all-to-all(bf16[32,17,2,128]{3,2,1,0:T(2,128)(2,1)S(1)} %bitcast.9), channel_id=1, replica_groups=mesh['slow'=8,'fast'=4] {'slow','fast'}, dimensions={0} | all-to-all | bytes 557056 | tf_op jit(solution)/shard_map/all_to_all | solution.py:447
  19.6 1.3 %group.1 = bf16[1088,128]{1,0:T(8,128)(2,1)S(1)} custom-call(bf16[1088,128]{1,0:T(8,128)(2,1)S(1)} %bitcast.7), custom_call_target="tpu_custom_call" | custom-call | tf_op jit(solution)/shard_map/group/pallas_call | solution.py:472
  20.9 0.0 copy-start
  20.9 0.0 copy-start.1
  21.0 0.0 copy-start.2
  21.0 0.0 copy-start.3
  21.0 13.1 %all_to_all.11 = bf16[32,17,2,128]{3,2,1,0:T(2,128)(2,1)S(1)} all-to-all(bf16[32,17,2,128]{3,2,1,0:T(2,128)(2,1)S(1)} %bitcast.8), channel_id=1, replica_groups=mesh['slow'=8,'fast'=4] {'slow','fast'}, dimensions={0} | all-to-all | bytes 557056 | tf_op jit(solution)/shard_map/all_to_all | solution.py:447
  34.1 0.0 copy-done
  34.1 0.0 copy-done.1
  34.1 0.0 copy-done.2
  34.1 0.0 copy-done.3
  34.1 1.0 %outputs.1 = (bf16[128,512]{1,0:T(8,128)(2,1)}, bf16[128,512]{1,0:T(8,128)(2,1)}, bf16[128,512]{1,0:T(8,128)(2,1)}, bf16[128,512]{1,0:T(8,128)(2,1)}, f32[32,128]{1,0:T(8,128)}) custom-call(bf16[1088,128]{1,0:T(8,128)(2,1)S(1)} %bitcast.6, bf16[128,512]{1,0:T(8,128)(2,1)S(1)} %copy-done, bf16[128,512]{1,0:T(8,128)(2,1)S(1)} %copy-done.1, ...), custom_call_target="tpu_custom_call" | custom-call | tf_op jit(solution)/shard_map/outputs/pallas_call | solution.py:485
Async XLA Ops:
  20.9 13.1 %copy-start = (bf16[128,512]{1,0:T(8,128)(2,1)S(1)}, bf16[128,512]{1,0:T(8,128)(2,1)}, u32[]{:S(2)}) copy-start(bf16[128,512]{1,0:T(8,128)(2,1)} %query.3) | copy-start | bytes 393220
  20.9 13.1 %copy-start.1 = (bf16[128,512]{1,0:T(8,128)(2,1)S(1)}, bf16[128,512]{1,0:T(8,128)(2,1)}, u32[]{:S(2)}) copy-start(bf16[128,512]{1,0:T(8,128)(2,1)} %key.3) | copy-start | bytes 393220
  21.0 13.1 %copy-start.2 = (bf16[128,512]{1,0:T(8,128)(2,1)S(1)}, bf16[128,512]{1,0:T(8,128)(2,1)}, u32[]{:S(2)}) copy-start(bf16[128,512]{1,0:T(8,128)(2,1)} %value.3) | copy-start | bytes 393220
  21.0 13.1 %copy-start.3 = (bf16[128,512]{1,0:T(8,128)(2,1)S(1)}, bf16[128,512]{1,0:T(8,128)(2,1)}, u32[]{:S(2)}) copy-start(bf16[128,512]{1,0:T(8,128)(2,1)} %grad.3) | copy-start | bytes 393220

commit v3 on v2

--- a/solution.py
+++ b/solution.py
@@ -344,24 +344,21 @@
     blocks = got.shape[0] // rows
     pairs = blocks // 2
     row, lane = ramp((tokens, tokens), 0), ramp((tokens, tokens), 1)
-    for pair in range(pairs):
-        for half in range(2):
-            block = 2 * pair + half
-            lanes = slice(half * tokens, (half + 1) * tokens)
-            at = 2 * width * pair
-            streams[at : at + width, lanes] = got[block * rows : block * rows + width, :]
-            streams[at + width : at + 2 * width, lanes] = got[
-                (blocks - 1 - block) * rows + width : (blocks - 1 - block) * rows + 2 * width, :
-            ]
+    loaded = []
     for block in range(blocks):
-        padded[block * width : (block + 1) * width, :] = got[
-            block * rows + width : block * rows + 2 * width, :
-        ]
+        mirror = blocks - 1 - block
+        here, there = (slice(half * tokens, (half + 1) * tokens) for half in (block % 2, mirror % 2))
+        product = got[block * rows : block * rows + width, :]
+        grad = got[block * rows + width : block * rows + 2 * width, :]
+        at = 2 * width * (block // 2)
+        streams[at : at + width, here] = product
+        at = 2 * width * (mirror // 2) + width
+        streams[at : at + width, there] = grad
+        padded[block * width : (block + 1) * width, :] = grad
+        loaded.append(product)
     padded[blocks * width :, :] = jnp.zeros((blocks * width, tokens), bf16)
 
-    ordered = jnp.concatenate(
-        [got[block * rows : block * rows + width, :] for block in range(blocks)], axis=0
-    )
+    ordered = jnp.concatenate(loaded, axis=0)
     ordered = ordered.astype(f32).T.astype(bf16)
     band = jnp.zeros((tokens, tokens), f32)
     before = jnp.zeros((tokens, tokens), f32)
@@ -400,16 +397,13 @@
         skip = 2 * width * pair
         term = dot(streams[0 : 2 * width * pairs - skip, :], weights)
         total = term if pair == 0 else jnp.concatenate((total[:skip], total[skip:] + term), axis=0)
-    for pair in range(pairs):
+        ready = total[skip : skip + 2 * width].astype(bf16)
         for half in range(2):
             block = 2 * pair + half
             lanes = slice(half * tokens, (half + 1) * tokens)
-            at = 2 * width * pair
-            sent[block * rows : block * rows + width, :] = total[at : at + width, lanes].astype(bf16)
+            sent[block * rows : block * rows + width, :] = ready[:width, lanes]
             place = (blocks - 1 - block) * rows + width
-            sent[place : place + width, :] = total[
-                at + width : at + 2 * width, lanes
-            ].astype(bf16)
+            sent[place : place + width, :] = ready[width:, lanes]
 
 
 def output_kernel(

time: 35.2 us -> 35.2 us (level)
  no operation moved by 1% of the time
where the time goes in v3:
time: 35.2 us; the launch traced here: 35 us
  blocking collectives  30.6 us (87%)
  Pallas kernels  3.68 us (10%)
  between operations  0.69 us (2%)
    all_to_all x2, blocking collectives, exchange(): lax.all_to_all(pieces, ('slow', 'fast'), split_axis=0, concat_axis=0, til...  30.6 us
    pallas_call x1, Pallas kernels, by_groups(): pl.pallas_call(gate_kernel, out_shape=chunks, in_specs=[pl.BlockSpec(memo...  1.42 us
    pallas_call x1, Pallas kernels, by_groups(): pl.pallas_call(functools.partial(group_kernel, scale, width), out_shape=c...  1.27 us
    pallas_call x1, Pallas kernels, by_groups(): pl.pallas_call(functools.partial(output_kernel, width), out_shape=(like,...  0.99 us

profile of v3, /device:TPU:1, one launch (start us, length us, event | category | flops | bytes accessed | tf_op | source)
XLA Modules:
  0.0 35.0 jit_solution(18180326384501993510)
XLA Ops:
  0.6 1.4 %gate.1 = bf16[1088,128]{1,0:T(8,128)(2,1)S(1)} custom-call(bf16[128,512]{1,0:T(8,128)(2,1)} %query.3, bf16[128,512]{1,0:T(8,128)(2,1)} %key.3, bf16[128,512]{1,0:T(8,128)(2,1)} %value.3, bf16[32,128]{1,0:T(8,128)(2,1)} %bitcast.10, bf16[128,512]{1,0:T(8,128)(2,1)} %grad.3), custom_call_target="tpu_custom_call" | custom-call | tf_op jit(solution)/shard_map/gate/pallas_call | solution.py:445
  2.1 17.6 %all_to_all.10 = bf16[32,17,2,128]{3,2,1,0:T(2,128)(2,1)S(1)} all-to-all(bf16[32,17,2,128]{3,2,1,0:T(2,128)(2,1)S(1)} %bitcast.9), channel_id=1, replica_groups=mesh['slow'=8,'fast'=4] {'slow','fast'}, dimensions={0} | all-to-all | bytes 557056 | tf_op jit(solution)/shard_map/all_to_all | solution.py:441
  19.6 1.3 %group.1 = bf16[1088,128]{1,0:T(8,128)(2,1)S(1)} custom-call(bf16[1088,128]{1,0:T(8,128)(2,1)S(1)} %bitcast.7), custom_call_target="tpu_custom_call" | custom-call | tf_op jit(solution)/shard_map/group/pallas_call | solution.py:466
  20.9 0.0 copy-start
  20.9 0.0 copy-start.1
  20.9 0.0 copy-start.2
  20.9 0.0 copy-start.3
  21.0 13.1 %all_to_all.11 = bf16[32,17,2,128]{3,2,1,0:T(2,128)(2,1)S(1)} all-to-all(bf16[32,17,2,128]{3,2,1,0:T(2,128)(2,1)S(1)} %bitcast.8), channel_id=1, replica_groups=mesh['slow'=8,'fast'=4] {'slow','fast'}, dimensions={0} | all-to-all | bytes 557056 | tf_op jit(solution)/shard_map/all_to_all | solution.py:441
  34.0 0.0 copy-done
  34.0 0.0 copy-done.1
  34.0 0.0 copy-done.2
  34.0 0.0 copy-done.3
  34.1 1.0 %outputs.1 = (bf16[128,512]{1,0:T(8,128)(2,1)}, bf16[128,512]{1,0:T(8,128)(2,1)}, bf16[128,512]{1,0:T(8,128)(2,1)}, bf16[128,512]{1,0:T(8,128)(2,1)}, f32[32,128]{1,0:T(8,128)}) custom-call(bf16[1088,128]{1,0:T(8,128)(2,1)S(1)} %bitcast.6, bf16[128,512]{1,0:T(8,128)(2,1)S(1)} %copy-done, bf16[128,512]{1,0:T(8,128)(2,1)S(1)} %copy-done.1, ...), custom_call_target="tpu_custom_call" | custom-call | tf_op jit(solution)/shard_map/outputs/pallas_call | solution.py:479
Async XLA Ops:
  20.9 13.1 %copy-start = (bf16[128,512]{1,0:T(8,128)(2,1)S(1)}, bf16[128,512]{1,0:T(8,128)(2,1)}, u32[]{:S(2)}) copy-start(bf16[128,512]{1,0:T(8,128)(2,1)} %query.3) | copy-start | bytes 393220
  20.9 13.1 %copy-start.1 = (bf16[128,512]{1,0:T(8,128)(2,1)S(1)}, bf16[128,512]{1,0:T(8,128)(2,1)}, u32[]{:S(2)}) copy-start(bf16[128,512]{1,0:T(8,128)(2,1)} %key.3) | copy-start | bytes 393220
  20.9 13.1 %copy-start.2 = (bf16[128,512]{1,0:T(8,128)(2,1)S(1)}, bf16[128,512]{1,0:T(8,128)(2,1)}, u32[]{:S(2)}) copy-start(bf16[128,512]{1,0:T(8,128)(2,1)} %value.3) | copy-start | bytes 393220
  20.9 13.1 %copy-start.3 = (bf16[128,512]{1,0:T(8,128)(2,1)S(1)}, bf16[128,512]{1,0:T(8,128)(2,1)}, u32[]{:S(2)}) copy-start(bf16[128,512]{1,0:T(8,128)(2,1)} %grad.3) | copy-start | bytes 393220

commit v4 on v2

--- a/solution.py
+++ b/solution.py
@@ -293,6 +293,10 @@
     return lax.dot_general(left, right, (((1,), (1,)), ((), ())), preferred_element_type=f32)
 
 
+def dot_tn(left, right):
+    return lax.dot_general(left, right, (((0,), (0,)), ((), ())), preferred_element_type=f32)
+
+
 def ramp(shape, dim):
     return lax.broadcasted_iota(jnp.int32, shape, dim)
 
@@ -303,6 +307,12 @@
 
 def eye_matrix(size):
     return (ramp((size, size), 0) == ramp((size, size), 1)).astype(bf16)
+
+
+def pair_matrix(count):
+    shape = (count, EXTRA_ROWS * count)
+    first = EXTRA_ROWS * ramp(shape, 0)
+    return ((ramp(shape, 1) >= first) & (ramp(shape, 1) < first + EXTRA_ROWS)).astype(bf16)
 
 
 def gate_kernel(query, key, value, filt, grad, sent, queries, keys, values, taps, grads, done):
@@ -325,14 +335,13 @@
     product = (keys[...].astype(f32) * values[...].astype(f32)).astype(bf16)
     columns = product.astype(f32).T.astype(bf16)
     flipped = flipped.T.astype(bf16)
+    doubled = dot_tn(pair_matrix(groups), taps[...]).astype(bf16)
     for group in range(groups):
         at = group * rows
         part = slice(group * width, (group + 1) * width)
         sent[at : at + width, :] = columns[part]
         sent[at + width : at + 2 * width, :] = flipped[part]
-        sent[at + 2 * width : at + rows, :] = jnp.broadcast_to(
-            taps[group : group + 1, :], (EXTRA_ROWS, tokens)
-        )
+        sent[at + 2 * width : at + rows, :] = doubled[EXTRA_ROWS * group : EXTRA_ROWS * (group + 1)]
 
 
 def turn(square):
@@ -430,8 +439,8 @@
     backward = dot_nt(flip, collect(width, width))
     key_grad[...] = (backward * value[...].astype(f32)).astype(bf16)
     value_grad[...] = (backward * key[...].astype(f32)).astype(bf16)
-    high, low = collect(2 * width, 1), collect(2 * width + 1, 1)
-    filter_grad[...] = dot(high, flip) + dot(low, flip)
+    turned = dot(collect(2 * width, EXTRA_ROWS), flip).astype(bf16)
+    filter_grad[...] = dot(pair_matrix(blocks), turned)
 
 
 def by_groups(query_act, key_act, value_act, long_filter, out_grad):

time: 35.2 us -> 35.3 us (level)
  no operation moved by 1% of the time
where the time goes in v4:
time: 35.3 us; the launch traced here: 35.1 us
  blocking collectives  30.6 us (87%)
  Pallas kernels  3.73 us (11%)
  between operations  0.69 us (2%)
    all_to_all x2, blocking collectives, exchange(): lax.all_to_all(pieces, ('slow', 'fast'), split_axis=0, concat_axis=0, til...  30.6 us
    pallas_call x1, Pallas kernels, by_groups(): pl.pallas_call(gate_kernel, out_shape=chunks, in_specs=[pl.BlockSpec(memo...  1.42 us
    pallas_call x1, Pallas kernels, by_groups(): pl.pallas_call(functools.partial(group_kernel, scale, width), out_shape=c...  1.29 us
    pallas_call x1, Pallas kernels, by_groups(): pl.pallas_call(functools.partial(output_kernel, width), out_shape=(like,...  1.03 us

profile of v4, /device:TPU:1, one launch (start us, length us, event | category | flops | bytes accessed | tf_op | source)
XLA Modules:
  0.0 35.1 jit_solution(17665166772927367295)
XLA Ops:
  0.6 1.4 %gate.1 = bf16[1088,128]{1,0:T(8,128)(2,1)S(1)} custom-call(bf16[128,512]{1,0:T(8,128)(2,1)} %query.3, bf16[128,512]{1,0:T(8,128)(2,1)} %key.3, bf16[128,512]{1,0:T(8,128)(2,1)} %value.3, bf16[32,128]{1,0:T(8,128)(2,1)} %bitcast.10, bf16[128,512]{1,0:T(8,128)(2,1)} %grad.3), custom_call_target="tpu_custom_call" | custom-call | tf_op jit(solution)/shard_map/gate/pallas_call | solution.py:460
  2.1 17.6 %all_to_all.10 = bf16[32,17,2,128]{3,2,1,0:T(2,128)(2,1)S(1)} all-to-all(bf16[32,17,2,128]{3,2,1,0:T(2,128)(2,1)S(1)} %bitcast.9), channel_id=1, replica_groups=mesh['slow'=8,'fast'=4] {'slow','fast'}, dimensions={0} | all-to-all | bytes 557056 | tf_op jit(solution)/shard_map/all_to_all | solution.py:456
  19.6 1.3 %group.1 = bf16[1088,128]{1,0:T(8,128)(2,1)S(1)} custom-call(bf16[1088,128]{1,0:T(8,128)(2,1)S(1)} %bitcast.7), custom_call_target="tpu_custom_call" | custom-call | tf_op jit(solution)/shard_map/group/pallas_call | solution.py:481
  20.9 0.0 copy-start
  20.9 0.0 copy-start.1
  20.9 0.0 copy-start.2
  21.0 0.0 copy-start.3
  21.0 13.1 %all_to_all.11 = bf16[32,17,2,128]{3,2,1,0:T(2,128)(2,1)S(1)} all-to-all(bf16[32,17,2,128]{3,2,1,0:T(2,128)(2,1)S(1)} %bitcast.8), channel_id=1, replica_groups=mesh['slow'=8,'fast'=4] {'slow','fast'}, dimensions={0} | all-to-all | bytes 557056 | tf_op jit(solution)/shard_map/all_to_all | solution.py:456
  34.0 0.0 copy-done
  34.0 0.0 copy-done.1
  34.0 0.0 copy-done.2
  34.1 0.0 copy-done.3
  34.1 1.0 %outputs.1 = (bf16[128,512]{1,0:T(8,128)(2,1)}, bf16[128,512]{1,0:T(8,128)(2,1)}, bf16[128,512]{1,0:T(8,128)(2,1)}, bf16[128,512]{1,0:T(8,128)(2,1)}, f32[32,128]{1,0:T(8,128)}) custom-call(bf16[1088,128]{1,0:T(8,128)(2,1)S(1)} %bitcast.6, bf16[128,512]{1,0:T(8,128)(2,1)S(1)} %copy-done, bf16[128,512]{1,0:T(8,128)(2,1)S(1)} %copy-done.1, ...), custom_call_target="tpu_custom_call" | custom-call | tf_op jit(solution)/shard_map/outputs/pallas_call | solution.py:494
Async XLA Ops:
  20.9 13.1 %copy-start = (bf16[128,512]{1,0:T(8,128)(2,1)S(1)}, bf16[128,512]{1,0:T(8,128)(2,1)}, u32[]{:S(2)}) copy-start(bf16[128,512]{1,0:T(8,128)(2,1)} %query.3) | copy-start | bytes 393220
  20.9 13.1 %copy-start.1 = (bf16[128,512]{1,0:T(8,128)(2,1)S(1)}, bf16[128,512]{1,0:T(8,128)(2,1)}, u32[]{:S(2)}) copy-start(bf16[128,512]{1,0:T(8,128)(2,1)} %key.3) | copy-start | bytes 393220
  20.9 13.1 %copy-start.2 = (bf16[128,512]{1,0:T(8,128)(2,1)S(1)}, bf16[128,512]{1,0:T(8,128)(2,1)}, u32[]{:S(2)}) copy-start(bf16[128,512]{1,0:T(8,128)(2,1)} %value.3) | copy-start | bytes 393220
  21.0 13.1 %copy-start.3 = (bf16[128,512]{1,0:T(8,128)(2,1)S(1)}, bf16[128,512]{1,0:T(8,128)(2,1)}, u32[]{:S(2)}) copy-start(bf16[128,512]{1,0:T(8,128)(2,1)} %grad.3) | copy-start | bytes 393220

commit v5 on v2

--- a/solution.py
+++ b/solution.py
@@ -299,10 +299,6 @@
 
 def flip_matrix(size):
     return (ramp((size, size), 0) + ramp((size, size), 1) == size - 1).astype(bf16)
-
-
-def eye_matrix(size):
-    return (ramp((size, size), 0) == ramp((size, size), 1)).astype(bf16)
 
 
 def gate_kernel(query, key, value, filt, grad, sent, queries, keys, values, taps, grads, done):
@@ -424,7 +420,7 @@
         )
 
     flip = flip_matrix(tokens)
-    convolved = dot_nt(eye_matrix(tokens), collect(0, width))
+    convolved = collect(0, width).astype(f32).T
     mixed[...] = (query[...].astype(f32) * convolved).astype(bf16)
     query_grad[...] = (grad[...].astype(f32) * convolved).astype(bf16)
     backward = dot_nt(flip, collect(width, width))

time: 35.2 us -> 35.3 us (level)
  no operation moved by 1% of the time
where the time goes in v5:
time: 35.3 us; the launch traced here: 35.1 us
  blocking collectives  30.6 us (87%)
  Pallas kernels  3.74 us (11%)
  between operations  0.69 us (2%)
    all_to_all x2, blocking collectives, exchange(): lax.all_to_all(pieces, ('slow', 'fast'), split_axis=0, concat_axis=0, til...  30.6 us
    pallas_call x1, Pallas kernels, by_groups(): pl.pallas_call(gate_kernel, out_shape=chunks, in_specs=[pl.BlockSpec(memo...  1.42 us
    pallas_call x1, Pallas kernels, by_groups(): pl.pallas_call(functools.partial(group_kernel, scale, width), out_shape=c...  1.29 us
    pallas_call x1, Pallas kernels, by_groups(): pl.pallas_call(functools.partial(output_kernel, width), out_shape=(like,...  1.03 us

profile of v5, /device:TPU:1, one launch (start us, length us, event | category | flops | bytes accessed | tf_op | source)
XLA Modules:
  0.0 35.1 jit_solution(17054067275777774747)
XLA Ops:
  0.6 1.4 %gate.1 = bf16[1088,128]{1,0:T(8,128)(2,1)S(1)} custom-call(bf16[128,512]{1,0:T(8,128)(2,1)} %query.3, bf16[128,512]{1,0:T(8,128)(2,1)} %key.3, bf16[128,512]{1,0:T(8,128)(2,1)} %value.3, bf16[32,128]{1,0:T(8,128)(2,1)} %bitcast.10, bf16[128,512]{1,0:T(8,128)(2,1)} %grad.3), custom_call_target="tpu_custom_call" | custom-call | tf_op jit(solution)/shard_map/gate/pallas_call | solution.py:447
  2.1 17.6 %all_to_all.10 = bf16[32,17,2,128]{3,2,1,0:T(2,128)(2,1)S(1)} all-to-all(bf16[32,17,2,128]{3,2,1,0:T(2,128)(2,1)S(1)} %bitcast.9), channel_id=1, replica_groups=mesh['slow'=8,'fast'=4] {'slow','fast'}, dimensions={0} | all-to-all | bytes 557056 | tf_op jit(solution)/shard_map/all_to_all | solution.py:443
  19.6 1.3 %group.1 = bf16[1088,128]{1,0:T(8,128)(2,1)S(1)} custom-call(bf16[1088,128]{1,0:T(8,128)(2,1)S(1)} %bitcast.7), custom_call_target="tpu_custom_call" | custom-call | tf_op jit(solution)/shard_map/group/pallas_call | solution.py:468
  20.9 0.0 copy-start
  20.9 0.0 copy-start.1
  21.0 0.0 copy-start.2
  21.0 0.0 copy-start.3
  21.0 13.1 %all_to_all.11 = bf16[32,17,2,128]{3,2,1,0:T(2,128)(2,1)S(1)} all-to-all(bf16[32,17,2,128]{3,2,1,0:T(2,128)(2,1)S(1)} %bitcast.8), channel_id=1, replica_groups=mesh['slow'=8,'fast'=4] {'slow','fast'}, dimensions={0} | all-to-all | bytes 557056 | tf_op jit(solution)/shard_map/all_to_all | solution.py:443
  34.1 0.0 copy-done
  34.1 0.0 copy-done.1
  34.1 0.0 copy-done.2
  34.1 0.0 copy-done.3
  34.1 1.0 %outputs.1 = (bf16[128,512]{1,0:T(8,128)(2,1)}, bf16[128,512]{1,0:T(8,128)(2,1)}, bf16[128,512]{1,0:T(8,128)(2,1)}, bf16[128,512]{1,0:T(8,128)(2,1)}, f32[32,128]{1,0:T(8,128)}) custom-call(bf16[1088,128]{1,0:T(8,128)(2,1)S(1)} %bitcast.6, bf16[128,512]{1,0:T(8,128)(2,1)S(1)} %copy-done, bf16[128,512]{1,0:T(8,128)(2,1)S(1)} %copy-done.1, ...), custom_call_target="tpu_custom_call" | custom-call | tf_op jit(solution)/shard_map/outputs/pallas_call | solution.py:481
Async XLA Ops:
  20.9 13.1 %copy-start = (bf16[128,512]{1,0:T(8,128)(2,1)S(1)}, bf16[128,512]{1,0:T(8,128)(2,1)}, u32[]{:S(2)}) copy-start(bf16[128,512]{1,0:T(8,128)(2,1)} %query.3) | copy-start | bytes 393220
  20.9 13.1 %copy-start.1 = (bf16[128,512]{1,0:T(8,128)(2,1)S(1)}, bf16[128,512]{1,0:T(8,128)(2,1)}, u32[]{:S(2)}) copy-start(bf16[128,512]{1,0:T(8,128)(2,1)} %key.3) | copy-start | bytes 393220
  21.0 13.1 %copy-start.2 = (bf16[128,512]{1,0:T(8,128)(2,1)S(1)}, bf16[128,512]{1,0:T(8,128)(2,1)}, u32[]{:S(2)}) copy-start(bf16[128,512]{1,0:T(8,128)(2,1)} %value.3) | copy-start | bytes 393220
  21.0 13.1 %copy-start.3 = (bf16[128,512]{1,0:T(8,128)(2,1)S(1)}, bf16[128,512]{1,0:T(8,128)(2,1)}, u32[]{:S(2)}) copy-start(bf16[128,512]{1,0:T(8,128)(2,1)} %grad.3) | copy-start | bytes 393220

commit v6 on v2

--- a/solution.py
+++ b/solution.py
@@ -339,7 +339,7 @@
     return pltpu.roll(square, 0, 1, stride=1, stride_axis=0)
 
 
-def group_kernel(scale, width, got, sent, streams, padded, toeplitz):
+def group_kernel(scale, width, got, sent, streams, padded):
     rows, tokens = 2 * width + EXTRA_ROWS, got.shape[1]
     blocks = got.shape[0] // rows
     pairs = blocks // 2
@@ -364,9 +364,17 @@
     )
     ordered = ordered.astype(f32).T.astype(bf16)
     band = jnp.zeros((tokens, tokens), f32)
+    left = jnp.zeros((tokens, tokens), bf16)
     before = jnp.zeros((tokens, tokens), f32)
     which = ramp((EXTRA_ROWS, tokens), 0)
+    total = None
     for pair in range(pairs):
+        bands = []
+        for block in (2 * pair, 2 * pair + 1):
+            taps = got[block * rows + 2 * width : block * rows + 2 * width + 1, :].astype(f32)
+            turned = turn(jnp.broadcast_to(taps, (tokens, tokens)))
+            bands.append(jnp.where(lane >= row, turned, band).astype(bf16))
+            band = turned
         depth = -(-2 * (pair + 1) * width // tokens) * tokens
         columns = [
             padded[pl.ds((blocks - 1 - lag) * width, depth), :] for lag in (2 * pair, 2 * pair + 1)
@@ -374,10 +382,6 @@
         outer = dot(ordered[:, :depth], jnp.concatenate(columns, axis=1))
         for half in range(2):
             block = 2 * pair + half
-            taps = got[block * rows + 2 * width : block * rows + 2 * width + 1, :].astype(f32)
-            turned = turn(jnp.broadcast_to(taps, (tokens, tokens)))
-            toeplitz[block] = jnp.where(lane >= row, turned, band).astype(bf16)
-            band = turned
             turned = turn(outer[:, half * tokens : (half + 1) * tokens])
             joined = jnp.where(lane >= row, turned, before)
             before = turned
@@ -386,17 +390,14 @@
             pieces = jnp.where(which == 0, high, value - high)
             place = (blocks - 1 - block) * rows + 2 * width
             sent[place : place + EXTRA_ROWS, :] = pieces.astype(bf16)
-
-    total = None
-    for pair in range(pairs):
-        left = jnp.zeros((tokens, tokens), bf16) if pair == 0 else toeplitz[2 * pair - 1]
         weights = jnp.concatenate(
             (
-                jnp.concatenate((toeplitz[2 * pair], toeplitz[2 * pair + 1]), axis=1),
-                jnp.concatenate((left, toeplitz[2 * pair]), axis=1),
+                jnp.concatenate((bands[0], bands[1]), axis=1),
+                jnp.concatenate((left, bands[0]), axis=1),
             ),
             axis=0,
         )
+        left = bands[1]
         skip = 2 * width * pair
         term = dot(streams[0 : 2 * width * pairs - skip, :], weights)
         total = term if pair == 0 else jnp.concatenate((total[:skip], total[skip:] + term), axis=0)
@@ -475,7 +476,6 @@
         scratch_shapes=[
             pltpu.VMEM((channels, 2 * tokens), bf16),
             pltpu.VMEM((2 * channels, tokens), bf16),
-            pltpu.VMEM((groups, tokens, tokens), bf16),
         ],
         compiler_params=pltpu.CompilerParams(vmem_limit_bytes=16 * 2**20),
         name="group",

time: 35.2 us -> 35.3 us (level)
  no operation moved by 1% of the time
where the time goes in v6:
time: 35.3 us; the launch traced here: 35.1 us
  blocking collectives  30.6 us (87%)
  Pallas kernels  3.77 us (11%)
  between operations  0.69 us (2%)
    all_to_all x2, blocking collectives, exchange(): lax.all_to_all(pieces, ('slow', 'fast'), split_axis=0, concat_axis=0, til...  30.6 us
    pallas_call x1, Pallas kernels, by_groups(): pl.pallas_call(gate_kernel, out_shape=chunks, in_specs=[pl.BlockSpec(memo...  1.42 us
    pallas_call x1, Pallas kernels, by_groups(): pl.pallas_call(functools.partial(group_kernel, scale, width), out_shape=c...  1.36 us
    pallas_call x1, Pallas kernels, by_groups(): pl.pallas_call(functools.partial(output_kernel, width), out_shape=(like,...  0.99 us

profile of v6, /device:TPU:1, one launch (start us, length us, event | category | flops | bytes accessed | tf_op | source)
XLA Modules:
  0.0 35.1 jit_solution(10751648235617308265)
XLA Ops:
  0.6 1.4 %gate.1 = bf16[1088,128]{1,0:T(8,128)(2,1)S(1)} custom-call(bf16[128,512]{1,0:T(8,128)(2,1)} %query.3, bf16[128,512]{1,0:T(8,128)(2,1)} %key.3, bf16[128,512]{1,0:T(8,128)(2,1)} %value.3, bf16[32,128]{1,0:T(8,128)(2,1)} %bitcast.10, bf16[128,512]{1,0:T(8,128)(2,1)} %grad.3), custom_call_target="tpu_custom_call" | custom-call | tf_op jit(solution)/shard_map/gate/pallas_call | solution.py:452
  2.1 17.6 %all_to_all.10 = bf16[32,17,2,128]{3,2,1,0:T(2,128)(2,1)S(1)} all-to-all(bf16[32,17,2,128]{3,2,1,0:T(2,128)(2,1)S(1)} %bitcast.9), channel_id=1, replica_groups=mesh['slow'=8,'fast'=4] {'slow','fast'}, dimensions={0} | all-to-all | bytes 557056 | tf_op jit(solution)/shard_map/all_to_all | solution.py:448
  19.6 1.4 %group.1 = bf16[1088,128]{1,0:T(8,128)(2,1)S(1)} custom-call(bf16[1088,128]{1,0:T(8,128)(2,1)S(1)} %bitcast.7), custom_call_target="tpu_custom_call" | custom-call | tf_op jit(solution)/shard_map/group/pallas_call | solution.py:473
  21.0 0.0 copy-start
  21.0 0.0 copy-start.1
  21.0 0.0 copy-start.2
  21.0 0.0 copy-start.3
  21.0 13.1 %all_to_all.11 = bf16[32,17,2,128]{3,2,1,0:T(2,128)(2,1)S(1)} all-to-all(bf16[32,17,2,128]{3,2,1,0:T(2,128)(2,1)S(1)} %bitcast.8), channel_id=1, replica_groups=mesh['slow'=8,'fast'=4] {'slow','fast'}, dimensions={0} | all-to-all | bytes 557056 | tf_op jit(solution)/shard_map/all_to_all | solution.py:448
  34.1 0.0 copy-done
  34.1 0.0 copy-done.1
  34.1 0.0 copy-done.2
  34.1 0.0 copy-done.3
  34.1 1.0 %outputs.1 = (bf16[128,512]{1,0:T(8,128)(2,1)}, bf16[128,512]{1,0:T(8,128)(2,1)}, bf16[128,512]{1,0:T(8,128)(2,1)}, bf16[128,512]{1,0:T(8,128)(2,1)}, f32[32,128]{1,0:T(8,128)}) custom-call(bf16[1088,128]{1,0:T(8,128)(2,1)S(1)} %bitcast.6, bf16[128,512]{1,0:T(8,128)(2,1)S(1)} %copy-done, bf16[128,512]{1,0:T(8,128)(2,1)S(1)} %copy-done.1, ...), custom_call_target="tpu_custom_call" | custom-call | tf_op jit(solution)/shard_map/outputs/pallas_call | solution.py:485
Async XLA Ops:
  21.0 13.1 %copy-start = (bf16[128,512]{1,0:T(8,128)(2,1)S(1)}, bf16[128,512]{1,0:T(8,128)(2,1)}, u32[]{:S(2)}) copy-start(bf16[128,512]{1,0:T(8,128)(2,1)} %query.3) | copy-start | bytes 393220
  21.0 13.1 %copy-start.1 = (bf16[128,512]{1,0:T(8,128)(2,1)S(1)}, bf16[128,512]{1,0:T(8,128)(2,1)}, u32[]{:S(2)}) copy-start(bf16[128,512]{1,0:T(8,128)(2,1)} %key.3) | copy-start | bytes 393220
  21.0 13.1 %copy-start.2 = (bf16[128,512]{1,0:T(8,128)(2,1)S(1)}, bf16[128,512]{1,0:T(8,128)(2,1)}, u32[]{:S(2)}) copy-start(bf16[128,512]{1,0:T(8,128)(2,1)} %value.3) | copy-start | bytes 393220
  21.0 13.1 %copy-start.3 = (bf16[128,512]{1,0:T(8,128)(2,1)S(1)}, bf16[128,512]{1,0:T(8,128)(2,1)}, u32[]{:S(2)}) copy-start(bf16[128,512]{1,0:T(8,128)(2,1)} %grad.3) | copy-start | bytes 393220
